TPU v7x, 32 devices: a whole 2x2x4 slice. The times are simulated.
32 devices in a mesh: groups: 2 (over x), tensor: 8 (over z, y), dp: 2 (over core).
Axes of the slice: x: 2, y: 2, z: 4, core: 2. Of those that a mesh axis runs over, the one named last changes fastest.
Arguments:
- activations: bfloat16 [512, 8192], P(('groups', 'dp'), 'tensor'), parts along dimension 0, may hold values from -640 to 640
- norm_gain: bfloat16 [8192], replicated, may hold values from 0.25 to 1.75
- gate_frozen_weight: bfloat16 [14336, 8192], P(('tensor', 'dp')), may hold values from -0.0625 to 0.0625
- up_frozen_weight: bfloat16 [14336, 8192], P(('tensor', 'dp')), may hold values from -0.0625 to 0.0625
- down_weight: bfloat16 [14336, 8192], P(('tensor', 'dp')), may hold values from -0.046875 to 0.046875
- cotangent: bfloat16 [512, 8192], P(('groups', 'dp'), 'tensor'), parts along dimension 0, may hold values from -6 to 6
- squeeze_master: float32 [256, 8192], P('groups', ('tensor', 'dp')), parts along dimension 0, may hold values from -0.0625 to 0.0625
- squeeze_first: float32 [256, 8192], P('groups', ('tensor', 'dp')), parts along dimension 0, may hold values from -100 to 100
- squeeze_second: float32 [256, 8192], P('groups', ('tensor', 'dp')), parts along dimension 0, may hold values from 100 to 2000
- expand_master: float32 [28672, 128], P(('groups', 'tensor', 'dp')), parts along dimension 0, may hold values from -0.75 to 0.75
- expand_first: float32 [28672, 128], P(('groups', 'tensor', 'dp')), parts along dimension 0, may hold values from -9 to 9
- expand_second: float32 [28672, 128], P(('groups', 'tensor', 'dp')), parts along dimension 0, may hold values from 0.5 to 10
Outputs:
- input_grad: float32 [512, 8192], P(('groups', 'dp'), 'tensor'), parts along dimension 0
- squeeze_master_new: float32 [256, 8192], P('groups', ('tensor', 'dp')), parts along dimension 0
- squeeze_first_new: float32 [256, 8192], P('groups', ('tensor', 'dp')), parts along dimension 0
- squeeze_second_new: float32 [256, 8192], P('groups', ('tensor', 'dp')), parts along dimension 0
- squeeze_adapter: bfloat16 [256, 8192], P('groups', 'tensor'), parts along dimension 0
- expand_master_new: float32 [28672, 128], P(('groups', 'tensor', 'dp')), parts along dimension 0
- expand_first_new: float32 [28672, 128], P(('groups', 'tensor', 'dp')), parts along dimension 0
- expand_second_new: float32 [28672, 128], P(('groups', 'tensor', 'dp')), parts along dimension 0
- expand_adapter: bfloat16 [28672, 128], P(('groups', 'tensor', 'dp')), parts along dimension 0
There are 2 independent parts, one for each index of `groups`. A program takes and returns all parts, laid end to end along the dimension named above; an argument that names none is the same for every part. Nothing has to cross between parts.
All inputs are finite; a program needn't handle non-finite values.
Results may differ from a plain program's by a relative error of at most 0.0055.
Values may be sent and summed in bfloat16 or wider, within the bound.
A program may use at most 128 MiB of HBM per device.

v0:
```python
import jax
import jax.numpy as jnp
from jax import lax
from jax.sharding import PartitionSpec as P

STEP = 20


adapter_output_scale = 0.25
norm_epsilon = 1e-05
learning_rate = 0.001
decay_rate = 0.1
beta_first = 0.9
beta_second = 0.95
adam_epsilon = 1e-08


def multiply_by_transpose(left, right):
    return lax.dot_general(
        left, right, (((1,), (1,)), ((), ())), preferred_element_type=jnp.float32
    )


def inner_rows(left, right):
    return lax.dot_general(
        left, right, (((0,), (0,)), ((), ())), preferred_element_type=jnp.float32
    )


def adamw_update(master, first, second, grads):
    first_new = beta_first * first + (1.0 - beta_first) * grads
    second_new = beta_second * second + (1.0 - beta_second) * grads * grads
    first_hat = first_new / (1.0 - beta_first**STEP)
    second_hat = second_new / (1.0 - beta_second**STEP)
    master_new = master - learning_rate * (
        first_hat / (jnp.sqrt(second_hat) + adam_epsilon) + decay_rate * master
    )
    return (master_new, first_new, second_new)


def on_device(
    activations,
    norm_gain,
    gate_frozen_weight,
    up_frozen_weight,
    down_weight,
    cotangent,
    squeeze_master,
    squeeze_first,
    squeeze_second,
    expand_master,
    expand_first,
    expand_second,
):
    model_width = norm_gain.shape[0]
    feature_slab = activations.shape[1]
    local_rows = activations.shape[0]
    adapter_inner_rank = expand_master.shape[1] // 2
    tensor_index = lax.axis_index("tensor")
    data_index = lax.axis_index("dp")
    gain_full = norm_gain.astype(jnp.float32)
    gain_slab = lax.dynamic_slice_in_dim(gain_full, tensor_index * feature_slab, feature_slab)
    squeeze_slab = lax.all_gather(squeeze_master.astype(jnp.bfloat16), "dp", axis=1, tiled=True)
    expand_factor_now = expand_master.astype(jnp.bfloat16)
    rows_input, rows_cotangent = (
        lax.all_gather(activations, "dp", axis=0, tiled=True),
        lax.all_gather(cotangent, "dp", axis=0, tiled=True),
    )
    rows_float = rows_input.astype(jnp.float32)
    square_part = jnp.sum(rows_float * rows_float, axis=1)
    square_total = lax.psum(square_part, "tensor")
    scale_rows = lax.rsqrt(square_total / model_width + norm_epsilon)
    normed_slab = (rows_float * scale_rows[:, None] * gain_slab).astype(jnp.bfloat16)
    shard_piece = lax.all_gather(normed_slab, "tensor", axis=1, tiled=True)
    gate_frozen_output = multiply_by_transpose(shard_piece, gate_frozen_weight)
    up_frozen_output = multiply_by_transpose(shard_piece, up_frozen_weight)
    low_part = multiply_by_transpose(normed_slab, squeeze_slab)
    reduced_features = lax.psum(low_part, "tensor").astype(jnp.bfloat16)
    gate_preactivation = gate_frozen_output + adapter_output_scale * multiply_by_transpose(
        reduced_features[:, :adapter_inner_rank], expand_factor_now[:, :adapter_inner_rank]
    )
    up_preactivation = up_frozen_output + adapter_output_scale * multiply_by_transpose(
        reduced_features[:, adapter_inner_rank:], expand_factor_now[:, adapter_inner_rank:]
    )
    hidden_grad = multiply_by_transpose(
        lax.all_gather(rows_cotangent, "tensor", axis=1, tiled=True), down_weight
    )
    sigmoid_gate = jax.nn.sigmoid(gate_preactivation)
    gate_branch_gradient = (
        hidden_grad
        * up_preactivation
        * sigmoid_gate
        * (1.0 + gate_preactivation * (1.0 - sigmoid_gate))
    ).astype(jnp.bfloat16)
    up_branch_gradient = (hidden_grad * gate_preactivation * sigmoid_gate).astype(jnp.bfloat16)
    reduced_piece_gradient = adapter_output_scale * jnp.concatenate(
        [
            jnp.dot(
                gate_branch_gradient,
                expand_factor_now[:, :adapter_inner_rank],
                preferred_element_type=jnp.float32,
            ),
            jnp.dot(
                up_branch_gradient,
                expand_factor_now[:, adapter_inner_rank:],
                preferred_element_type=jnp.float32,
            ),
        ],
        axis=1,
    )
    low_sum = lax.psum(reduced_piece_gradient, ("tensor", "dp"))
    reduced_gradient = low_sum.astype(jnp.bfloat16)
    row_block = lax.psum_scatter(
        jnp.dot(gate_branch_gradient, gate_frozen_weight, preferred_element_type=jnp.float32)
        + jnp.dot(up_branch_gradient, up_frozen_weight, preferred_element_type=jnp.float32),
        "dp",
        scatter_dimension=0,
        tiled=True,
    )
    normed_grad = lax.psum_scatter(row_block, "tensor", scatter_dimension=1, tiled=True)
    own_rows = data_index * local_rows
    low_own = lax.dynamic_slice_in_dim(reduced_gradient, own_rows, local_rows, 0)
    normed_grad = normed_grad + jnp.dot(low_own, squeeze_slab, preferred_element_type=jnp.float32)
    scale_own = lax.dynamic_slice_in_dim(scale_rows, own_rows, local_rows)
    input_float = activations.astype(jnp.float32)
    row_total = lax.psum(jnp.sum(normed_grad * input_float * gain_slab, axis=1), "tensor")
    input_grad = (
        scale_own[:, None] * gain_slab * normed_grad
        - input_float * (scale_own**3)[:, None] * row_total[:, None] / model_width
    )
    master_cols = squeeze_master.shape[1]
    normed_cols = lax.dynamic_slice_in_dim(normed_slab, data_index * master_cols, master_cols, 1)
    squeeze_grad = inner_rows(reduced_gradient, normed_cols)
    expand_factor_gradient = adapter_output_scale * jnp.concatenate(
        [
            inner_rows(gate_branch_gradient, reduced_features[:, :adapter_inner_rank]),
            inner_rows(up_branch_gradient, reduced_features[:, adapter_inner_rank:]),
        ],
        axis=1,
    )
    squeeze_new, squeeze_first_new, squeeze_second_new = adamw_update(
        squeeze_master, squeeze_first, squeeze_second, squeeze_grad
    )
    expand_new, expand_first_new, expand_second_new = adamw_update(
        expand_master, expand_first, expand_second, expand_factor_gradient
    )
    squeeze_adapter = lax.all_gather(squeeze_new.astype(jnp.bfloat16), "dp", axis=1, tiled=True)
    return (
        input_grad,
        squeeze_new,
        squeeze_first_new,
        squeeze_second_new,
        squeeze_adapter,
        expand_new,
        expand_first_new,
        expand_second_new,
        expand_new.astype(jnp.bfloat16),
    )


def solution(mesh):
    placed = (
        P(("groups", "dp"), "tensor"),
        P(),
        P(("tensor", "dp"), None),
        P(("tensor", "dp"), None),
        P(("tensor", "dp"), None),
        P(("groups", "dp"), "tensor"),
        P("groups", ("tensor", "dp")),
        P("groups", ("tensor", "dp")),
        P("groups", ("tensor", "dp")),
        P(("groups", "tensor", "dp"), None),
        P(("groups", "tensor", "dp"), None),
        P(("groups", "tensor", "dp"), None),
    )
    return jax.shard_map(
        on_device,
        mesh=mesh,
        in_specs=placed,
        out_specs=(
            P(("groups", "dp"), "tensor"),
            P("groups", ("tensor", "dp")),
            P("groups", ("tensor", "dp")),
            P("groups", ("tensor", "dp")),
            P("groups", "tensor"),
            P(("groups", "tensor", "dp"), None),
            P(("groups", "tensor", "dp"), None),
            P(("groups", "tensor", "dp"), None),
            P(("groups", "tensor", "dp"), None),
        ),
        check_vma=False,
    )
```

profile of v0, /device:TPU:0, one launch (start us, length us, event | category | flops | bytes accessed | tf_op | source)
XLA Modules:
  0.0 354.4 jit_solution(14602233168791047449)
XLA Ops:
  7.2 0.0 all-gather.5.cloned.1.call-start
  7.2 2.5 all_gather.18
  9.7 0.2 fusion.6
  9.9 23.0 %psum.28 = f32[256]{0:T(256)S(1)} all-reduce(f32[256]{0:T(256)S(1)} %fusion.6), channel_id=1, replica_groups=mesh['groups'=2,'tensor'=8,'dp'=2] {'tensor'}, use_global_device_ids=true, to_apply=%region_1.0 | all-reduce | flops 256 | bytes 2048 | tf_op jit(solution)/shard_map/psum | solution.py:71
  32.9 0.7 dynamic-slice_convert_fusion
  33.6 1.0 fusion.8
  34.6 0.0 all-gather.5.cloned.1.call-update
  34.6 0.0 all-gather.3.cloned.1.call-start
  34.7 3.8 %all_gather.19 = bf16[256,1024]{1,0:T(8,128)(2,1)} all-gather(bf16[128,1024]{1,0:T(8,128)(2,1)} %param.17), channel_id=1, replica_groups=mesh['groups'=2,'tensor'=8,'dp'=2] {'dp'}, dimensions={0}, use_global_device_ids=true | all-gather | bytes 786432 | tf_op jit(solution)/shard_map/all_gather | solution.py:67
  38.5 0.0 all-gather.3.cloned.1.call-update
  38.5 0.0 reduce-scatter.3.cloned.1.call-start
  38.6 1.0 convert_element_type.39
  39.6 2.0 all_gather.22
  41.6 1.3 fusion.36
  42.9 1.0 convert_element_type.41
  44.0 36.6 %all-reduce.2 = bf16[256,128]{1,0:T(8,128)(2,1)S(1)} all-reduce(f32[256,128]{1,0:T(8,128)S(1)} %fusion.36), channel_id=1, replica_groups=mesh['groups'=2,'tensor'=8,'dp'=2] {'tensor'}, use_global_device_ids=true, to_apply=%region_2.0 | all-reduce | flops 32768 | bytes 196608 | tf_op jit(solution)/shard_map/psum | solution.py:78
  80.6 27.1 %all-gather.5.cloned.1.call-done = bf16[256,8192]{1,0:T(8,128)(2,1)} async-done(((bf16[256,1024]{1,0:T(8,128)(2,1)}), bf16[256,8192]{1,0:T(8,128)(2,1)}) %all-gather.5.cloned.1.call-update) | async-done | bytes 4194320 | tf_op jit(solution)/shard_map/all_gather | solution.py:74
  107.7 11.2 %fusion.37 = f32[256,896]{1,0:T(8,128)S(1)} fusion(bf16[256,8192]{1,0:T(8,128)(2,1)} %all-gather.5.cloned.1.call-done, bf16[896,8192]{1,0:T(8,128)(2,1)} %param.14), kind=kOutput, calls=%fused_computation.57 | convolution fusion | flops 3758096384 | bytes 19791872 | tf_op jit(solution)/shard_map/dot_general | solution.py:19
  118.9 0.3 fusion
  119.2 12.0 %fusion.35 = f32[256,896]{1,0:T(8,128)} fusion(bf16[256,8192]{1,0:T(8,128)(2,1)} %all-gather.5.cloned.1.call-done, bf16[896,8192]{1,0:T(8,128)(2,1)} %param.15), kind=kOutput, calls=%fused_computation.55 | convolution fusion | flops 3758096384 | bytes 19791872 | tf_op jit(solution)/shard_map/dot_general | solution.py:19
  131.2 50.9 %all-gather.3.cloned.1.call-done = bf16[256,8192]{1,0:T(8,128)(2,1)} async-done(((bf16[256,1024]{1,0:T(8,128)(2,1)}), bf16[256,8192]{1,0:T(8,128)(2,1)}) %all-gather.3.cloned.1.call-update) | async-done | bytes 4194320 | tf_op jit(solution)/shard_map/all_gather | solution.py:86
  182.1 11.7 %multiply_convert_fusion = (bf16[256,896]{1,0:T(8,128)(2,1)S(1)}, f32[256,896]{1,0:T(8,128)S(1)}) fusion(f32[256,896]{1,0:T(8,128)S(1)} %fusion, bf16[256,8192]{1,0:T(8,128)(2,1)} %all-gather.3.cloned.1.call-done, bf16[896,8192]{1,0:T(8,128)(2,1)} %param.16), kind=kOutput, calls=%fused_computation.15 | convolution fusion | flops 3759472640 | bytes 21168128 | tf_op jit(solution)/shard_map/dot_general | solution.py:19
  193.8 0.6 fusion.5
  194.5 8.0 %fusion.38 = f32[256,8192]{1,0:T(8,128)S(1)} fusion(bf16[256,896]{1,0:T(8,128)(2,1)S(1)} %fusion.5, bf16[896,8192]{1,0:T(8,128)(2,1)} %param.14), kind=kOutput, calls=%fused_computation.58 | convolution fusion | flops 3758096384 | bytes 23527424 | tf_op jit(solution)/shard_map/dot_general | solution.py:114
  202.5 12.1 %convolution_add_fusion = f32[256,8192]{1,0:T(8,128)} fusion(f32[256,8192]{1,0:T(8,128)S(1)} %fusion.38, bf16[256,896]{1,0:T(8,128)(2,1)S(1)} %get-tuple-element.28, bf16[896,8192]{1,0:T(8,128)(2,1)} %param.15), kind=kOutput, calls=%fused_computation | convolution fusion | flops 3760193536 | bytes 31916032 | tf_op jit(solution)/shard_map/dot_general | solution.py:115
  214.6 0.0 reduce-scatter.5.cloned.1.call-start
  214.7 15.2 %reduce-scatter.3.cloned.1.call-done = f32[128,8192]{1,0:T(8,128)} async-done(((f32[256,8192]{1,0:T(8,128)}), f32[128,8192]{1,0:T(8,128)}) %reduce-scatter.3.cloned.1.call-update) | async-done | bytes 4194320 | tf_op jit(solution)/shard_map/reduce_scatter | solution.py:113
  229.9 0.2 copy.24
  230.1 1.2 copy.21
  231.3 2.0 copy.22
  233.3 0.1 multiply_multiply_fusion.1
  233.4 0.3 fusion.17
  233.6 0.4 fusion.20
  234.1 0.2 fusion.23
  234.3 0.3 fusion.26
  234.6 2.2 fusion.32
  236.8 2.0 copy.25
  238.8 1.0 copy.26
  239.8 1.0 copy.27
  240.7 0.8 copy.28
  241.6 65.8 %all-reduce.3 = bf16[256,128]{0,1:T(8,128)(2,1)S(1)} all-reduce(f32[256,128]{0,1:T(8,128)S(1)} %maximum_multiply_fusion), channel_id=1, replica_groups=mesh['groups'=2,'tensor'=8,'dp'=2] {'tensor','dp'}, use_global_device_ids=true, to_apply=%region_5.0 | all-reduce | flops 32768 | bytes 196608 | tf_op jit(solution)/shard_map/psum | solution.py:111
  307.4 2.3 fusion.33
  309.7 2.0 all_gather.23
  311.7 12.9 %reduce-scatter.5.cloned.1.call-done = f32[128,1024]{1,0:T(8,128)} async-done(((f32[128,8192]{1,0:T(8,128)}), f32[128,1024]{1,0:T(8,128)}) %reduce-scatter.5.cloned.1.call-update) | async-done | bytes 524304 | tf_op jit(solution)/shard_map/reduce_scatter | solution.py:120
  324.6 1.4 fusion.13
  325.9 20.2 %psum.31 = f32[128]{0:T(128)S(1)} all-reduce(f32[128]{0:T(128)S(1)} %get-tuple-element.30), channel_id=1, replica_groups=mesh['groups'=2,'tensor'=8,'dp'=2] {'tensor'}, use_global_device_ids=true, to_apply=%region_7.0 | all-reduce | flops 128 | bytes 1024 | tf_op jit(solution)/shard_map/psum | solution.py:126
  346.1 1.0 fusion.11
  347.1 0.7 copy.34
  (12 shorter events, 0.1 us)
Async XLA Ops:
  7.2 100.5 %all-gather.5.cloned.1.call-start = ((), (), s32[]{:S(2)}) async-start(), calls=%async_computation.3 | async-start | bytes 4718592 | tf_op jit(solution)/shard_map/all_gather | solution.py:74
  34.6 147.5 %all-gather.3.cloned.1.call-start = ((), (), s32[]{:S(2)}) async-start(), calls=%async_computation.2 | async-start | bytes 4718592 | tf_op jit(solution)/shard_map/all_gather | solution.py:86
  38.5 191.3 %reduce-scatter.3.cloned.1.call-start = ((), (), s32[]{:S(2)}) async-start(), calls=%async_computation.4 | async-start | bytes 12582912 | tf_op jit(solution)/shard_map/reduce_scatter | solution.py:113
  182.1 11.7 %copy-start.3 = (f32[256,896]{1,0:T(8,128)S(1)}, f32[256,896]{1,0:T(8,128)}, u32[]{:S(2)}) copy-start(f32[256,896]{1,0:T(8,128)} %fusion.35) | copy-start | bytes 2752516
  202.4 27.4 %copy-start.2 = (f32[896,128]{1,0:T(8,128)S(1)}, f32[896,128]{1,0:T(8,128)}, u32[]{:S(2)}) copy-start(f32[896,128]{1,0:T(8,128)} %param.21) | copy-start | bytes 1376260
  214.6 92.8 %copy-start = (bf16[256,1024]{1,0:T(8,128)(2,1)S(1)}, bf16[256,1024]{1,0:T(8,128)(2,1)}, u32[]{:S(2)}) copy-start(bf16[256,1024]{1,0:T(8,128)(2,1)} %fusion.8) | copy-start | bytes 1572868
  214.6 110.0 %copy-start.1 = (bf16[128,1024]{1,0:T(8,128)(2,1)S(1)}, bf16[128,1024]{1,0:T(8,128)(2,1)}, u32[]{:S(2)}) copy-start(bf16[128,1024]{1,0:T(8,128)(2,1)} %param.12) | copy-start | bytes 786436
  214.6 110.0 %reduce-scatter.5.cloned.1.call-start = ((), (), s32[]{:S(2)}) async-start(), calls=%async_computation.5 | async-start | bytes 4718592 | tf_op jit(solution)/shard_map/reduce_scatter | solution.py:120
Sparse Core Ops, SparseCore 0:
  34.8 72.9 all-gather.4
  109.9 72.1 all-gather.2
  214.7 15.0 reduce-scatter.2
  233.8 90.7 reduce-scatter.4
where the time goes:
time: 355 us; the launch traced here: 354 us
  blocking collectives  156 us (44%)
  waiting for transfers between devices  106 us (30%)
  matrix products  62.2 us (18%)
  between operations  13.9 us (4%)
  local copies, waits for them, and re-layouts  8.87 us (2%)
  other arithmetic  7.18 us (2%)
    psum x1, blocking collectives, on_device(): low_sum = lax.psum(reduced_piece_gradient, ('tensor', 'dp'))  65.8 us
    all_gather x1, waiting for transfers between devices, on_device(): lax.all_gather(rows_cotangent, 'tensor', axis=1, tiled=True)  50.9 us
    dot_general x6, matrix products, multiply_by_transpose(): lax.dot_general(left, right, (((1,), (1,)), ((), ())), preferred_element_...  37.1 us
    psum x1, blocking collectives, on_device(): reduced_features = lax.psum(low_part, 'tensor').astype(jnp.bfloat16)  36.6 us
    all_gather x1, waiting for transfers between devices, on_device(): shard_piece = lax.all_gather(normed_slab, 'tensor', axis=1, tiled=True)  27.1 us
    psum x1, blocking collectives, on_device(): square_total = lax.psum(square_part, 'tensor')  23 us
    psum x1, blocking collectives, on_device(): lax.psum(jnp.sum(normed_grad * input_float * gain_slab, axis=1), 'tensor')  20.2 us
    reduce_scatter x1, waiting for transfers between devices, on_device(): lax.psum_scatter(jnp.dot(gate_branch_gradient, gate_frozen_weight, prefer...  15.2 us
  transfers between devices with their start and end apart: 4, of which 4 were waited for; matrix products, arithmetic and copies ran while one was open for 12% of the time, Pallas kernels for 0%

commit v1 on v0

v1 whole, which is shorter than its diff:
```python
import functools

import jax
import jax.numpy as jnp
from jax import lax
from jax.experimental import pallas as pl
from jax.experimental.pallas import tpu as pltpu
from jax.sharding import PartitionSpec as P

STEP = 20
MESH = pl.DeviceIdType.MESH
F32 = jnp.float32
BF16 = jnp.bfloat16

adapter_output_scale = 0.25
norm_epsilon = 1e-05
learning_rate = 0.001
decay_rate = 0.1
beta_first = 0.9
beta_second = 0.95
adam_epsilon = 1e-08


def dot_t(left, right):
    return lax.dot_general(left, right, (((1,), (1,)), ((), ())), preferred_element_type=F32)


def dot_rows(left, right):
    return lax.dot_general(left, right, (((0,), (0,)), ((), ())), preferred_element_type=F32)


def dot_n(left, right):
    return jnp.dot(left, right, preferred_element_type=F32)


def adamw_update(master, first, second, grads):
    first_new = beta_first * first + (1.0 - beta_first) * grads
    second_new = beta_second * second + (1.0 - beta_second) * grads * grads
    first_hat = first_new / (1.0 - beta_first**STEP)
    second_hat = second_new / (1.0 - beta_second**STEP)
    master_new = master - learning_rate * (
        first_hat / (jnp.sqrt(second_hat) + adam_epsilon) + decay_rate * master
    )
    return (master_new, first_new, second_new)


def layer_kernel(
    T,
    act, cot, gain, wg, wu, wd, sqm, sqf, sqs, exm, exf, exs,
    out_grad, o_sqm, o_sqf, o_sqs, o_sqa, o_exm, o_exf, o_exs, o_exa,
    G, WG, WU, HID, AG, AU, GG, UG, EX, EB, SQ, SQV, SC, LOW, LGP, LGR, LGF,
    YS4, YR4, ZS4, ZR4, PO, CSS, CSR, YS, YR, ZS, ZR, SQA, EA,
    sG, rG, wsem, lsem, osem, sSib, rSib, sY4, rY4, sZ4, rZ4,
    sCS, rCS, sYR, rYR, sZR, rZR,
):
    Z = T // 2
    n = 2 * Z - 1
    S = act.shape[1]
    H = wg.shape[0]
    rows = act.shape[0]
    width = S * T
    Q = sqm.shape[1]
    me = lax.axis_index("tensor")
    c = lax.axis_index("dp")
    z = me // 2
    y = me % 2
    sib = {"tensor": me, "dp": 1 - c}
    yp = {"tensor": z * 2 + (1 - y), "dp": c}

    def zdev(zz):
        return {"tensor": zz * 2 + y, "dp": c}

    def rc(src, dst, ss, rs, dev):
        return pltpu.make_async_remote_copy(
            src_ref=src, dst_ref=dst, send_sem=ss, recv_sem=rs,
            device_id=dev, device_id_type=MESH,
        )

    def item(i):
        d = (i + 1) // 2
        zz = z + (2 * (i % 2) - 1) * d
        return zz, jnp.logical_and(zz >= 0, zz < Z)

    def wcopy(m, t):
        src = (wg, wu, wd)[m]
        dst = (WG, WU, WU)[m]
        return pltpu.make_async_copy(
            src.at[:, pl.ds(pl.multiple_of(t * S, S), S)], dst.at[t], wsem.at[m, t]
        )

    ex_in = (exm, exf, exs)
    sq_in = (sqm, sqf, sqs)
    ex_out = (o_exm, o_exf, o_exs)
    sq_out = (o_sqm, o_sqf, o_sqs)
    sq_load = [pltpu.make_async_copy(sq_in[k], SQV.at[k], lsem.at[k]) for k in range(3)]
    ex_load = [pltpu.make_async_copy(ex_in[k], EX.at[k], lsem.at[3 + k]) for k in range(3)]
    for cp in sq_load + ex_load:
        cp.start()

    barrier = pltpu.get_barrier_semaphore()
    pl.semaphore_signal(barrier, inc=1, device_id=sib, device_id_type=MESH)
    pl.semaphore_signal(barrier, inc=1, device_id=yp, device_id_type=MESH)

    @pl.loop(1, Z)
    def _(j):
        pl.semaphore_signal(barrier, inc=1, device_id=zdev((z + j) % Z), device_id_type=MESH)

    def load_weights(m):
        @pl.loop(0, n)
        def _(i):
            zz, ok = item(i)

            @pl.when(ok)
            def _():
                wcopy(m, zz * 2 + y).start()
                wcopy(m, zz * 2 + 1 - y).start()

    load_weights(2)
    load_weights(0)

    G[0, me, c] = cot[...]
    xf = act[...].astype(F32)
    YS4[0] = jnp.broadcast_to(jnp.sum(xf * xf, axis=1, keepdims=True), (rows, 128))
    pl.semaphore_wait(barrier, Z + 1)

    def ar_y(k):
        return rc(YS4.at[k], YR4.at[k], sY4.at[k], rY4.at[k], yp)

    def ar_z(k, j):
        return rc(ZS4.at[k], ZR4.at[k, z], sZ4.at[k, j], rZ4.at[k, z], zdev((z + j) % Z))

    def ar_mid(k):
        ar_y(k).wait_recv()
        ZS4[k] = YS4[k] + YR4[k]

        @pl.loop(1, Z)
        def _(j):
            ar_z(k, j).start()

    def ar_end(k):
        YR4[k] = ZS4[k]

        @pl.loop(1, Z)
        def _(j):
            o = (z + j) % Z
            rc(ZS4.at[k], ZR4.at[k, o], sZ4.at[k, j], rZ4.at[k, o], zdev(o)).wait_recv()
            YR4[k] = YR4[k] + ZR4[k, o]

        return YR4[k]

    def ar_drain(k):
        ar_y(k).wait_send()

        @pl.loop(1, Z)
        def _(j):
            ar_z(k, j).wait_send()

    def slot_send(a, t, k, dev):
        return rc(G.at[a, t, c], G.at[a, t, c], sG.at[a, t, k], rG.at[a, t, c], dev)

    def slot_recv(a, t, cc):
        rc(G.at[a, t, cc], G.at[a, t, cc], sG.at[a, t, 0], rG.at[a, t, cc], sib).wait_recv()

    def forward(a, zz, op):
        t = zz * 2 + y

        @pl.when(jnp.logical_and(zz <= z, z + 1 < Z))
        def _():
            op(slot_send(a, t, 0, zdev(z + 1)))

        @pl.when(jnp.logical_and(zz >= z, z > 0))
        def _():
            op(slot_send(a, t, 1, zdev(z - 1)))

        op(slot_send(a, t, 2, yp))
        op(slot_send(a, t, 3, sib))

    def begin(cp):
        cp.start()

    ar_y(0).start()
    forward(0, z, begin)
    sq_load[0].wait()
    SQ[c] = SQV[0].astype(BF16)
    sq_send = rc(SQ.at[c], SQ.at[c], sSib.at[0], rSib.at[0], sib)
    sq_send.start()
    HID[...] = jnp.zeros_like(HID)
    AG[...] = jnp.zeros_like(AG)
    AU[...] = jnp.zeros_like(AU)
    ar_mid(0)
    SC[...] = lax.rsqrt(ar_end(0) / width + norm_epsilon)
    G[1, me, c] = (act[...].astype(F32) * SC[:, :1] * gain[...]).astype(BF16)
    forward(1, z, begin)
    rc(SQ.at[1 - c], SQ.at[1 - c], sSib.at[0], rSib.at[0], sib).wait_recv()
    own = G[1, me, c]
    YS4[1] = dot_t(own[:, :Q], SQ[0]) + dot_t(own[:, Q:], SQ[1])
    ar_y(1).start()

    low_send = rc(LOW.at[c], LOW.at[c], sSib.at[1], rSib.at[1], sib)

    @pl.loop(0, 2 * n + 3)
    def _(g):
        @pl.when(g < 2 * n)
        def _():
            a, i = g // n, g % n
            zz, ok = item(i)

            @pl.when(jnp.logical_and(ok, i > 0))
            def _():
                slot_recv(a, zz * 2 + y, c)
                forward(a, zz, begin)

        @pl.when(jnp.logical_and(g >= 2, g < 2 * n + 2))
        def _():
            a, i = (g - 2) // n, (g - 2) % n
            zz, ok = item(i)

            @pl.when(ok)
            def _():
                t = zz * 2 + 1 - y
                slot_recv(a, t, c)
                slot_send(a, t, 3, sib).start()

        @pl.when(g >= 3)
        def _():
            a, i = (g - 3) // n, (g - 3) % n
            zz, ok = item(i)

            @pl.when(ok)
            def _():
                @pl.loop(0, 2)
                def _(r):
                    t = zz * 2 + (y + r) % 2
                    slot_recv(a, t, 1 - c)

                    @pl.when(a == 0)
                    def _():
                        wcopy(2, t).wait()
                        block = G[0, t].reshape(2 * rows, S)
                        HID[...] += dot_t(block, WU[t])
                        wcopy(1, t).start()

                    @pl.when(a == 1)
                    def _():
                        block = G[1, t].reshape(2 * rows, S)
                        wcopy(0, t).wait()
                        AG[...] += dot_t(block, WG[t])
                        wcopy(1, t).wait()
                        AU[...] += dot_t(block, WU[t])

        @pl.when(g == 2)
        def _():
            ar_mid(1)

        @pl.when(g == n)
        def _():
            LOW[c] = ar_end(1).astype(BF16)
            low_send.start()

    rc(LOW.at[1 - c], LOW.at[1 - c], sSib.at[1], rSib.at[1], sib).wait_recv()
    for cp in ex_load:
        cp.wait()
    EB[...] = EX[0].astype(BF16)
    rank = EB.shape[1] // 2
    chunk = 64
    per = rows // chunk

    @pl.loop(0, 2 * per)
    def _(q):
        h, r = q // per, q % per
        inner = pl.ds(pl.multiple_of(r * chunk, chunk), chunk)
        sl = pl.ds(pl.multiple_of(q * chunk, chunk), chunk)
        low = LOW[h, inner]
        left = lax.broadcasted_iota(jnp.int32, low.shape, 1) < rank
        zero = jnp.zeros_like(low)
        b = EB[...]
        gate = AG[sl] + adapter_output_scale * dot_t(jnp.where(left, low, zero), b)
        up = AU[sl] + adapter_output_scale * dot_t(jnp.where(left, zero, low), b)
        hid = HID[sl]
        s = jax.nn.sigmoid(gate)
        gg = (hid * up * s * (1.0 + gate * (1.0 - s))).astype(BF16)
        ug = (hid * gate * s).astype(BF16)
        GG[sl] = gg
        UG[sl] = ug
        LGP[h, 0, inner] = adapter_output_scale * jnp.where(left, dot_n(gg, b), dot_n(ug, b))
        dots = jnp.sum(gg.astype(F32) * gate + ug.astype(F32) * up, axis=1, keepdims=True)
        LGP[h, 1, inner] = jnp.broadcast_to(dots, (chunk, 128))

    lg_send = rc(LGP.at[1 - c], LGR, sSib.at[2], rSib.at[2], sib)
    lg_send.start()
    lgf_send = rc(LGF.at[c], LGF.at[c], sSib.at[3], rSib.at[3], sib)

    def cs_copy(t):
        return rc(CSS.at[t], CSR.at[t], sCS.at[t], rCS.at[t], sib)

    def yr_copy(zz):
        return rc(YS.at[zz], YR.at[zz], sYR.at[zz], rYR.at[zz], yp)

    def right_copy(zz):
        return rc(ZS.at[zz], ZR.at[0, zz], sZR.at[zz], rZR.at[0, zz], zdev(z + 1))

    def left_copy(zz):
        return rc(ZS.at[zz], ZR.at[1, zz], sZR.at[zz], rZR.at[1, zz], zdev(z - 1))

    def chain_recv(way, zz):
        rc(ZS.at[zz], ZR.at[way, zz], sZR.at[zz], rZR.at[way, zz], sib).wait_recv()

    def chain(zz):
        t = zz * 2 + y
        yr_copy(zz).wait_recv()
        PO[t] = PO[t] + YR[zz].astype(F32)

        @pl.when(jnp.logical_and(zz >= z, z > 0))
        def _():
            chain_recv(0, zz)
            PO[t] = PO[t] + ZR[0, zz].astype(F32)

        @pl.when(jnp.logical_and(zz <= z, z + 1 < Z))
        def _():
            chain_recv(1, zz)
            PO[t] = PO[t] + ZR[1, zz].astype(F32)

        @pl.when(zz > z)
        def _():
            ZS[zz] = PO[t].astype(BF16)
            right_copy(zz).start()

        @pl.when(zz < z)
        def _():
            ZS[zz] = PO[t].astype(BF16)
            left_copy(zz).start()

    @pl.loop(0, 2 * n + 2)
    def _(g):
        @pl.when(g < 2 * n)
        def _():
            p, i = g // n, n - 1 - g % n
            zz, ok = item(i)

            @pl.when(ok)
            def _():
                t = zz * 2 + (1 - y + p) % 2
                part = dot_n(GG[...], WG[t]) + dot_n(UG[...], WU[t])
                part = part.reshape(2, rows, S)

                @pl.when(c == 0)
                def _():
                    PO[t] = part[0]
                    CSS[t] = part[1].astype(BF16)

                @pl.when(c == 1)
                def _():
                    PO[t] = part[1]
                    CSS[t] = part[0].astype(BF16)

                cs_copy(t).start()

        @pl.when(jnp.logical_and(g >= 1, g < 2 * n + 1))
        def _():
            p, i = (g - 1) // n, n - 1 - (g - 1) % n
            zz, ok = item(i)

            @pl.when(ok)
            def _():
                t = zz * 2 + (1 - y + p) % 2
                cs_copy(t).wait_recv()
                PO[t] = PO[t] + CSR[t].astype(F32)

                @pl.when(p == 0)
                def _():
                    YS[zz] = PO[t].astype(BF16)
                    yr_copy(zz).start()

        @pl.when(g >= n + 2)
        def _():
            i = n - 1 - (g - n - 2)
            zz, ok = item(i)

            @pl.when(jnp.logical_and(ok, i > 0))
            def _():
                chain(zz)

        @pl.when(g == 2)
        def _():
            lg_send.wait_recv()
            YS4[2] = LGP[c, 0] + LGR[0]
            YS4[3] = LGP[c, 1] + LGR[1]
            ar_y(2).start()
            ar_y(3).start()

        @pl.when(g == n - 1)
        def _():
            ar_mid(2)
            ar_mid(3)

        @pl.when(g == n + 2)
        def _():
            LGF[c] = ar_end(2).astype(BF16)
            lgf_send.start()

    low = LOW[...].reshape(2 * rows, 2 * rank)
    left = lax.broadcasted_iota(jnp.int32, low.shape, 1) < rank
    zero = jnp.zeros_like(low)
    grads = adapter_output_scale * (
        dot_rows(GG[...], jnp.where(left, low, zero)) + dot_rows(UG[...], jnp.where(left, zero, low))
    )
    new = adamw_update(EX[0], EX[1], EX[2], grads)
    for k in range(3):
        EX[k] = new[k]
    EA[...] = new[0].astype(BF16)
    stores = [pltpu.make_async_copy(EX.at[k], ex_out[k], osem.at[k]) for k in range(3)]
    stores.append(pltpu.make_async_copy(EA, o_exa, osem.at[3]))
    for cp in stores:
        cp.start()
    for cp in sq_load[1:]:
        cp.wait()
    rc(LGF.at[1 - c], LGF.at[1 - c], sSib.at[3], rSib.at[3], sib).wait_recv()
    cols = pl.ds(pl.multiple_of(c * Q, Q), Q)
    sgrads = dot_rows(LGF[0], G[1, me, 0, :, cols]) + dot_rows(LGF[1], G[1, me, 1, :, cols])
    snew = adamw_update(SQV[0], SQV[1], SQV[2], sgrads)
    for k in range(3):
        SQV[k] = snew[k]
    SQA[c] = snew[0].astype(BF16)
    sqa_send = rc(SQA.at[c], SQA.at[c], sSib.at[4], rSib.at[4], sib)
    sqa_send.start()
    more = [pltpu.make_async_copy(SQV.at[k], sq_out[k], osem.at[4 + k]) for k in range(3)]
    for cp in more:
        cp.start()
    row_dot = ar_end(3)[:, :1]
    chain(z)
    lo = LGF[c]
    scale = SC[:, :1]
    for k in range(2):
        fs = slice(k * Q, (k + 1) * Q)
        ng = PO[me, :, fs] + dot_n(lo, SQ[k])
        out_grad[:, fs] = scale * gain[:, fs] * ng - act[:, fs].astype(F32) * (
            scale * scale * row_dot / width
        )
    rc(SQA.at[1 - c], SQA.at[1 - c], sSib.at[4], rSib.at[4], sib).wait_recv()
    for k in range(2):
        o_sqa[:, k * Q:(k + 1) * Q] = SQA[k]

    for cp in stores + more:
        cp.wait()
    for cp in (sq_send, low_send, lg_send, lgf_send, sqa_send):
        cp.wait_send()
    for k in range(4):
        ar_drain(k)

    def sent(cp):
        cp.wait_send()

    @pl.loop(0, Z)
    def _(zz):
        for a in range(2):
            forward(a, zz, sent)
            slot_send(a, zz * 2 + 1 - y, 3, sib).wait_send()
        cs_copy(zz * 2).wait_send()
        cs_copy(zz * 2 + 1).wait_send()
        yr_copy(zz).wait_send()

        @pl.when(zz > z)
        def _():
            right_copy(zz).wait_send()

        @pl.when(zz < z)
        def _():
            left_copy(zz).wait_send()


def on_device(
    T, activations, norm_gain, gate, up, down, cotangent,
    sqm, sqf, sqs, exm, exf, exs,
):
    rows, S = activations.shape
    H = gate.shape[0]
    Z = T // 2
    ranks, Q = sqm.shape
    index = lax.axis_index("tensor")
    gain = lax.dynamic_slice_in_dim(norm_gain, index * S, S).astype(F32)[None, :]
    vmem = pl.BlockSpec(memory_space=pltpu.VMEM)
    hbm = pl.BlockSpec(memory_space=pl.ANY)
    DMA = pltpu.SemaphoreType.DMA
    V = pltpu.VMEM
    shape = jax.ShapeDtypeStruct
    return pl.pallas_call(
        functools.partial(layer_kernel, T),
        out_shape=(
            shape((rows, S), F32), shape(sqm.shape, F32), shape(sqm.shape, F32),
            shape(sqm.shape, F32), shape((ranks, 2 * Q), BF16), shape(exm.shape, F32),
            shape(exm.shape, F32), shape(exm.shape, F32), shape(exm.shape, BF16),
        ),
        in_specs=[vmem, vmem, vmem] + [hbm] * 9,
        out_specs=(vmem, hbm, hbm, hbm, vmem, hbm, hbm, hbm, hbm),
        scratch_shapes=[
            V((2, T, 2, rows, S), BF16),
            V((T, H, S), BF16), V((T, H, S), BF16),
            V((2 * rows, H), F32), V((2 * rows, H), F32), V((2 * rows, H), F32),
            V((2 * rows, H), BF16), V((2 * rows, H), BF16),
            V((3,) + exm.shape, F32), V(exm.shape, BF16),
            V((2, ranks, Q), BF16), V((3, ranks, Q), F32),
            V((rows, 128), F32),
            V((2, rows, ranks), BF16), V((2, 2, rows, 128), F32), V((2, rows, 128), F32),
            V((2, rows, ranks), BF16),
            V((4, rows, 128), F32), V((4, rows, 128), F32), V((4, rows, 128), F32),
            V((4, Z, rows, 128), F32),
            V((T, rows, S), F32), V((T, rows, S), BF16), V((T, rows, S), BF16),
            V((Z, rows, S), BF16), V((Z, rows, S), BF16), V((Z, rows, S), BF16),
            V((2, Z, rows, S), BF16),
            V((2, ranks, Q), BF16), V(exm.shape, BF16),
            DMA((2, T, 4)), DMA((2, T, 2)), DMA((3, T)), DMA((6,)), DMA((8,)),
            DMA((5,)), DMA((5,)), DMA((4,)), DMA((4,)), DMA((4, Z)), DMA((4, Z)),
            DMA((T,)), DMA((T,)), DMA((Z,)), DMA((Z,)), DMA((Z,)), DMA((2, Z)),
        ],
        compiler_params=pltpu.CompilerParams(
            collective_id=0, has_side_effects=True, vmem_limit_bytes=63 * 2**20
        ),
    )(activations, cotangent, gain, gate, up, down, sqm, sqf, sqs, exm, exf, exs)


def solution(mesh):
    rows = P(("groups", "dp"), "tensor")
    hidden = P(("tensor", "dp"), None)
    sq = P("groups", ("tensor", "dp"))
    ex = P(("groups", "tensor", "dp"), None)
    return jax.shard_map(
        functools.partial(on_device, mesh.shape["tensor"]),
        mesh=mesh,
        in_specs=(rows, P(), hidden, hidden, hidden, rows, sq, sq, sq, ex, ex, ex),
        out_specs=(rows, sq, sq, sq, P("groups", "tensor"), ex, ex, ex, ex),
        check_vma=False,
    )
```

time: 355 us -> 136 us (0.38)
  blocking collectives: 156 us -> 0 us
  Pallas kernels: 0 us -> 118 us
  waiting for transfers between devices: 106 us -> 0 us
  matrix products: 62.2 us -> 0 us
  between operations: 13.9 us -> 0.66 us
  local copies, waits for them, and re-layouts: 8.87 us -> 15.6 us
  other arithmetic: 7.18 us -> 1.28 us
    psum x4 -> x0, blocking collectives: 146 us -> none  [the longest x1 65.8 us: on_device(): low_sum = lax.psum(reduced_piece_gradient, ('tensor', 'dp'))]
    pallas_call x0 -> x1, Pallas kernels: none -> 118 us  [on_device(): pl.pallas_call(functools.partial(layer_kernel, T), out_shape=(shape((rows...]
    all_gather x2 -> x0, waiting for transfers between devices: 78 us -> none  [the longest x1 50.9 us: on_device(): lax.all_gather(rows_cotangent, 'tensor', axis=1, tiled=True)]
    dot_general x14 -> x0, matrix products: 62.2 us -> none  [the longest x6 37.1 us: multiply_by_transpose(): lax.dot_general(left, right, (((1,), (1,)), ((), ())), preferred_element_...]
    reduce_scatter x2 -> x0, waiting for transfers between devices: 28 us -> none  [the longest x1 15.2 us: on_device(): lax.psum_scatter(jnp.dot(gate_branch_gradient, gate_frozen_weight, prefer...]
    all_gather x4 -> x0, blocking collectives: 10.3 us -> none  [the longest x1 3.84 us: on_device(): lax.all_gather(cotangent, 'dp', axis=0, tiled=True)]
    unnamed x16 -> x9, local copies, waits for them, and re-layouts: 8.87 us -> 15.6 us
    convert_element_type x5 -> x0, other arithmetic: 5.88 us -> none  [the longest x1 2.18 us: on_device(): expand_new.astype(jnp.bfloat16)]
  transfers between devices with their start and end apart: 4 -> 0, of which waited for: 4 -> 0; matrix products, arithmetic and copies ran while one was open for 12% -> 0% of each run, Pallas kernels for 0% -> 0%
where the time goes in v1:
time: 136 us
  Pallas kernels  118 us (87%)
  local copies, waits for them, and re-layouts  15.6 us (11%)
    pallas_call x1, Pallas kernels, on_device(): pl.pallas_call(functools.partial(layer_kernel, T), out_shape=(shape((rows...  118 us
    unnamed x9, local copies, waits for them, and re-layouts  15.6 us

profile of v1, /device:TPU:0, one launch (start us, length us, event | category | flops | bytes accessed | tf_op | source)
XLA Modules:
  0.0 135.6 jit_solution(8954614005029083657)
XLA Ops:
  0.6 1.3 dynamic-slice_convert_fusion
  1.9 118.0 %shard_map.187 = (f32[128,1024]{1,0:T(8,128)}, f32[128,512]{1,0:T(8,128)}, f32[128,512]{1,0:T(8,128)}, f32[128,512]{1,0:T(8,128)}, bf16[128,1024]{1,0:T(8,128)(2...) custom-call(bf16[128,1024]{1,0:T(8,128)(2,1)} %act.1, ...), custom_call_target="tpu_custom_call" | custom-call | tf_op jit(solution)/shard_map/pallas_call | solution.py:486
  119.9 1.9 %copy.30 = f32[128,1024]{1,0:T(8,128)} copy(f32[128,1024]{1,0:T(8,128)} %get-tuple-element.18) | data formatting | bytes 1048576
  121.8 1.7 %copy.31 = f32[128,512]{1,0:T(8,128)} copy(f32[128,512]{1,0:T(8,128)} %get-tuple-element.19) | data formatting | bytes 524288
  123.5 1.7 %copy.32 = f32[128,512]{1,0:T(8,128)} copy(f32[128,512]{1,0:T(8,128)} %get-tuple-element.20) | data formatting | bytes 524288
  125.2 1.7 %copy.33 = f32[128,512]{1,0:T(8,128)} copy(f32[128,512]{1,0:T(8,128)} %get-tuple-element.21) | data formatting | bytes 524288
  126.8 1.7 %copy.34 = bf16[128,1024]{1,0:T(8,128)(2,1)} copy(bf16[128,1024]{1,0:T(8,128)(2,1)} %get-tuple-element.22) | data formatting | bytes 524288
  128.5 1.8 %copy.35 = f32[896,128]{1,0:T(8,128)} copy(f32[896,128]{1,0:T(8,128)} %get-tuple-element.23) | data formatting | bytes 917504
  130.3 1.8 %copy.36 = f32[896,128]{1,0:T(8,128)} copy(f32[896,128]{1,0:T(8,128)} %get-tuple-element.24) | data formatting | bytes 917504
  132.1 1.8 %copy.37 = f32[896,128]{1,0:T(8,128)} copy(f32[896,128]{1,0:T(8,128)} %get-tuple-element.25) | data formatting | bytes 917504
  133.9 1.6 %copy.38 = bf16[896,128]{1,0:T(8,128)(2,1)} copy(bf16[896,128]{1,0:T(8,128)(2,1)} %get-tuple-element.26) | data formatting | bytes 458752
